TPU v7x, 32 devices: a whole 2x2x4 slice. The times are simulated.
32 devices in a mesh: groups: 2 (over y), rows: 8 (over z, x), cols: 1, sub: 2 (over core).
Axes of the slice: x: 2, y: 2, z: 4, core: 2. Of those that a mesh axis runs over, the one named last changes fastest.
Arguments:
- points: float32 [256, 65536], P('cols', ('groups', 'rows', 'sub')), parts along dimension 1, may hold values from -17 to 17
- start_block: float32 [256, 64], P('cols'), may hold values from -6 to 6
- median_order: int32 [32, 2048], P(('groups', 'rows', 'sub')), parts along dimension 0, may hold values from 0 to 2047, each once within a row
Outputs:
- moved_points: float32 [256, 65536], P('cols', ('groups', 'rows', 'sub')), parts along dimension 1
- moved_coords: float32 [64, 65536], P(None, ('groups', 'rows', 'sub')), parts along dimension 1
There are 2 independent parts, one for each index of `groups`. A program takes and returns all parts, laid end to end along the dimension named above; an argument that names none is the same for every part. Nothing has to cross between parts.
Inputs may be any that keep to these rules, and one draw needn't show every extreme that they name: `median_order`: each row is a permutation of the local positions.
All inputs are finite; a program needn't handle non-finite values.
Results may differ from a plain program's by a relative error of at most 0.00016.
Values sent between devices are 32-bit elements; how exact they have to be, the bound alone decides.
A program may use at most 64 MiB of HBM per device.

v0:
```python
import jax
import jax.numpy as jnp
from jax import lax
from jax.sharding import PartitionSpec as P

ITERS = 3


HI = lax.Precision.HIGHEST


def orthonormal(wblock, gram):
    lower = jnp.linalg.cholesky(gram)
    return jax.scipy.linalg.solve_triangular(lower, wblock.T, lower=True).T


def weighted(points, coords, scale):
    return lax.dot_general(points, coords, (((1,), (1,)), ((), ())), precision=HI) * scale


def body(points, start_block, median_order):
    total = points.shape[1] * lax.axis_size("rows") * lax.axis_size("sub")
    scale = 1.0 / total
    coords = None

    def project(block):
        return lax.psum(jnp.dot(block.T, points, precision=HI), "cols")

    block = start_block
    for step in range(ITERS):
        coords = project(block)
        partial_value = weighted(points, coords, scale)
        wblock = lax.psum(partial_value, ("rows", "sub"))
        gram = lax.psum(jnp.dot(wblock.T, wblock, precision=HI), "cols")
        block = orthonormal(wblock, gram)
    coords = project(block)
    order = median_order[0]
    sent_points = jnp.take(points, order, axis=1)
    sent_coords = jnp.take(coords, order, axis=1)
    moved_points, moved_coords = (
        lax.all_to_all(sent_points, "rows", split_axis=1, concat_axis=1, tiled=True),
        lax.all_to_all(sent_coords, "rows", split_axis=1, concat_axis=1, tiled=True),
    )
    return (moved_points, moved_coords)


def solution(mesh):
    in_specs = (
        P("cols", ("groups", "rows", "sub")),
        P("cols", None),
        P(("groups", "rows", "sub"), None),
    )
    out_specs = (P("cols", ("groups", "rows", "sub")), P(None, ("groups", "rows", "sub")))
    return jax.shard_map(body, mesh=mesh, in_specs=in_specs, out_specs=out_specs, check_vma=False)
```

profile of v0, /device:TPU:0, one launch (start us, length us, event | category | flops | bytes accessed | tf_op | source)
XLA Modules:
  0.0 415.0 jit_solution(14471720603312446105)
XLA Ops:
  7.2 0.0 copy-start
  7.2 0.0 copy-start.1
  7.2 0.0 copy-start.2
  7.2 0.0 all-reduce.4.cloned.1.call-start
  7.2 0.8 copy-done
  8.0 3.0 fusion.22
  11.0 0.0 copy-done.1
  11.0 2.7 fusion.2
  13.6 0.0 all-reduce.4.cloned.1.call-update
  13.7 0.0 all-reduce.6.cloned.1.call-start
  13.7 0.0 copy-done.2
  13.7 87.1 %all-reduce.4.cloned.1.call-done = f32[256,64]{0,1:T(8,128)} async-done(((f32[256,64]{0,1:T(8,128)}), f32[256,64]{0,1:T(8,128)}) %all-reduce.4.cloned.1.call-update) | async-done | bytes 65552 | tf_op jit(solution)/shard_map/psum | solution.py:33
  100.9 1.1 fusion.23
  102.0 0.1 copy.28
  102.1 5.8 %cholesky.59 = f32[64,64]{1,0:T(8,128)S(1)} custom-call(f32[64,64]{1,0:T(8,128)S(1)} %fusion.17), custom_call_target="Cholesky" | custom-call | tf_op jit(solution)/shard_map/jit(cholesky)/cholesky | solution.py:13
  108.0 0.6 compare_reduce_fusion.2
  108.6 0.7 fusion.9
  109.3 4.9 %custom-call.7 = f32[1,64,64]{1,2,0:T(8,128)S(1)} custom-call(f32[1,64,64]{2,1,0:T(8,128)S(1)} %fusion.9), custom_call_target="InvertDiagBlocksLowerTriangular" | custom-call | tf_op jit(solution)/shard_map/jit(_solve_triangular)/triangular_solve | solution.py:14
  114.2 1.1 fusion.7
  115.3 1.4 fusion.24
  116.7 2.7 fusion.1
  119.4 0.0 all-reduce.6.cloned.1.call-update
  119.4 0.2 all-reduce.8.cloned.1.call-start
  119.6 0.5 broadcast.90
  120.1 0.7 reduce.7
  120.8 84.8 %all-reduce.6.cloned.1.call-done = f32[256,64]{0,1:T(8,128)} async-done(((f32[256,64]{0,1:T(8,128)}), f32[256,64]{0,1:T(8,128)}) %all-reduce.6.cloned.1.call-update) | async-done | bytes 65552 | tf_op jit(solution)/shard_map/psum | solution.py:33
  205.6 1.1 fusion.25
  206.7 0.1 copy.29
  206.8 5.8 %cholesky.70 = f32[64,64]{1,0:T(8,128)S(1)} custom-call(f32[64,64]{1,0:T(8,128)S(1)} %fusion.15), custom_call_target="Cholesky" | custom-call | tf_op jit(solution)/shard_map/jit(cholesky)/cholesky | solution.py:13
  212.7 0.6 compare_reduce_fusion.1
  213.3 0.7 fusion.10
  214.0 4.9 %custom-call.8 = f32[1,64,64]{1,2,0:T(8,128)S(1)} custom-call(f32[1,64,64]{2,1,0:T(8,128)S(1)} %fusion.10), custom_call_target="InvertDiagBlocksLowerTriangular" | custom-call | tf_op jit(solution)/shard_map/jit(_solve_triangular)/triangular_solve | solution.py:14
  218.9 1.1 fusion.5
  220.0 1.4 fusion.26
  221.4 2.7 fusion
  224.0 0.0 all-reduce.8.cloned.1.call-update
  224.1 86.2 %all-reduce.8.cloned.1.call-done = f32[256,64]{0,1:T(8,128)} async-done(((f32[256,64]{0,1:T(8,128)}), f32[256,64]{0,1:T(8,128)}) %all-reduce.8.cloned.1.call-update) | async-done | bytes 65552 | tf_op jit(solution)/shard_map/psum | solution.py:33
  310.3 1.1 fusion.27
  311.4 0.1 copy.30
  311.5 5.8 %cholesky.81 = f32[64,64]{1,0:T(8,128)S(1)} custom-call(f32[64,64]{1,0:T(8,128)S(1)} %fusion.13), custom_call_target="Cholesky" | custom-call | tf_op jit(solution)/shard_map/jit(cholesky)/cholesky | solution.py:13
  317.4 0.6 compare_reduce_fusion
  318.0 0.7 fusion.11
  318.7 4.9 %custom-call.9 = f32[1,64,64]{1,2,0:T(8,128)S(1)} custom-call(f32[1,64,64]{2,1,0:T(8,128)S(1)} %fusion.11), custom_call_target="InvertDiagBlocksLowerTriangular" | custom-call | tf_op jit(solution)/shard_map/jit(_solve_triangular)/triangular_solve | solution.py:14
  323.6 1.1 fusion.3
  324.7 3.4 fusion.28
  328.1 5.5 %gather_fusion.1 = f32[2048,64]{1,0:T(8,128)S(1)} fusion(f32[64,2048]{0,1:T(8,128)S(1)} %fusion.28, s32[2048]{0:T(1024)S(1)} %broadcast_clamp_fusion), kind=kCustom, calls=%fused_computation.1 | custom fusion | bytes 1056768 | tf_op jit(solution)/shard_map/jit(_take)/gather | solution.py:39
  333.6 0.3 copy.32
  333.9 0.8 broadcast_select_fusion.1
  334.8 6.2 %all-to-all-start.1 = ((f32[64,8,256]{2,0,1:T(8,128)}), f32[64,8,256]{2,0,1:T(8,128)S(1)}, u32[]{:S(2)}, u32[]{:S(2)}) async-start(f32[64,8,256]{2,0,1:T(8,128)} %broadcast_select_fusion.1), calls=%async_computation.1 | async-start | bytes 1048576 | tf_op jit(solution)/shard_map/all_to_all | solution.py:42
  341.0 1.9 copy.26
  342.9 8.6 %gather_fusion = f32[2048,256]{1,0:T(8,128)} fusion(f32[256,2048]{0,1:T(8,128)S(1)} %copy.26, s32[2048]{0:T(1024)S(1)} %broadcast_clamp_fusion), kind=kCustom, calls=%fused_computation | custom fusion | bytes 4202496 | tf_op jit(solution)/shard_map/jit(_take)/gather | solution.py:38
  351.5 3.2 broadcast_select_fusion
  354.7 0.0 all-to-all-done.1
  354.7 6.0 %all-to-all-start = ((f32[256,8,256]{0,2,1:T(8,128)}), f32[256,8,256]{0,2,1:T(8,128)S(1)}, u32[]{:S(2)}, u32[]{:S(2)}) async-start(f32[256,8,256]{0,2,1:T(8,128)} %broadcast_select_fusion), calls=%async_computation | async-start | bytes 4194304 | tf_op jit(solution)/shard_map/all_to_all | solution.py:41
  360.7 0.8 copy.36
  361.6 45.1 %all-to-all-done = f32[256,8,256]{0,2,1:T(8,128)S(1)} async-done(((f32[256,8,256]{0,2,1:T(8,128)}), f32[256,8,256]{0,2,1:T(8,128)S(1)}, u32[]{:S(2)}, u32[]{:S(2)}) %all-to-all-start) | async-done | bytes 2097184 | tf_op jit(solution)/shard_map/all_to_all | solution.py:41
  406.7 1.8 copy.35
  (10 shorter events, 0.1 us)
Async XLA Ops:
  7.2 0.8 copy-start
  7.2 3.8 copy-start.1
  7.2 6.5 %copy-start.2 = (s32[1,2048]{1,0:T(1,128)S(1)}, s32[1,2048]{1,0:T(1,128)}, u32[]{:S(2)}) copy-start(s32[1,2048]{1,0:T(1,128)} %param.8) | copy-start | bytes 24580
  7.2 93.7 %all-reduce.4.cloned.1.call-start = ((), (), s32[]{:S(2)}) async-start(), calls=%async_computation.2 | async-start | bytes 131072 | tf_op jit(solution)/shard_map/psum | solution.py:33
  13.7 191.9 %all-reduce.6.cloned.1.call-start = ((), (), s32[]{:S(2)}) async-start(), calls=%async_computation.3 | async-start | bytes 131072 | tf_op jit(solution)/shard_map/psum | solution.py:33
  119.4 190.9 %all-reduce.8.cloned.1.call-start = ((), (), s32[]{:S(2)}) async-start(), calls=%async_computation.4 | async-start | bytes 131072 | tf_op jit(solution)/shard_map/psum | solution.py:33
  334.8 20.0 %all-to-all-start.1 = ((f32[64,8,256]{2,0,1:T(8,128)}), f32[64,8,256]{2,0,1:T(8,128)S(1)}, u32[]{:S(2)}, u32[]{:S(2)}) async-start(f32[64,8,256]{2,0,1:T(8,128)} %broadcast_select_fusion.1), calls=%async_computation.1 | async-start | bytes 1048576 | tf_op jit(solution)/shard_map/all_to_all | solution.py:42
  354.7 51.9 %all-to-all-start = ((f32[256,8,256]{0,2,1:T(8,128)}), f32[256,8,256]{0,2,1:T(8,128)S(1)}, u32[]{:S(2)}, u32[]{:S(2)}) async-start(f32[256,8,256]{0,2,1:T(8,128)} %broadcast_select_fusion), calls=%async_computation | async-start | bytes 4194304 | tf_op jit(solution)/shard_map/all_to_all | solution.py:41
Sparse Core Ops, SparseCore 0:
  13.8 87.0 all-reduce.3
  119.5 86.0 all-reduce.5
  224.2 86.0 all-reduce.7
where the time goes:
time: 416 us; the launch traced here: 415 us
  waiting for transfers between devices  303 us (73%)
  other arithmetic  41 us (10%)
  matrix products  23.8 us (6%)
  local copies, waits for them, and re-layouts  20.5 us (5%)
  between operations  14 us (3%)
  starting transfers between devices  12.5 us (3%)
    psum x3, waiting for transfers between devices, body(): wblock = lax.psum(partial_value, ('rows', 'sub'))  258 us
    all_to_all x1, waiting for transfers between devices, body(): lax.all_to_all(sent_points, 'rows', split_axis=1, concat_axis=1, tiled=True)  45.1 us
    another operation x9, other arithmetic, orthonormal(): lower = jnp.linalg.cholesky(gram)  19.6 us
    another operation x6, other arithmetic, orthonormal(): return jax.scipy.linalg.solve_triangular(lower, wblock.T, lower=True).T  16.6 us
    dot_general x4, matrix products, project(): return lax.psum(jnp.dot(block.T, points, precision=HI), 'cols')  9.15 us
    gather x1, local copies, waits for them, and re-layouts, body(): sent_points = jnp.take(points, order, axis=1)  8.61 us
  transfers between devices with their start and end apart: 5, of which 4 were waited for; matrix products, arithmetic and copies ran while one was open for 4% of the time, Pallas kernels for 0%

commit v1 on v0

--- a/solution.py
+++ b/solution.py
@@ -1,12 +1,17 @@
+import functools
 import jax
 import jax.numpy as jnp
 from jax import lax
+from jax.experimental import pallas as pl
+from jax.experimental.pallas import tpu as pltpu
 from jax.sharding import PartitionSpec as P
 
 ITERS = 3
 
 
 HI = lax.Precision.HIGHEST
+MESH = pl.DeviceIdType.MESH
+NT = (((1,), (1,)), ((), ()))
 
 
 def orthonormal(wblock, gram):
@@ -15,7 +20,7 @@
 
 
 def weighted(points, coords, scale):
-    return lax.dot_general(points, coords, (((1,), (1,)), ((), ())), precision=HI) * scale
+    return lax.dot_general(points, coords, NT, precision=HI) * scale
 
 
 def body(points, start_block, median_order):
@@ -44,6 +49,178 @@
     return (moved_points, moved_coords)
 
 
+def eliminate(gram, wide):
+    size = gram.shape[0]
+    done = []
+    for base in range(0, size, 8):
+        rows = lax.broadcasted_iota(jnp.int32, (gram.shape[0], 1), 0)
+        for kk in range(8):
+            k = base + kk
+            row_g = gram[kk : kk + 1, :]
+            inv = 1.0 / row_g[:, k : k + 1]
+            col = jnp.where(rows > kk, gram[:, k : k + 1], 0.0)
+            row_w = wide[kk : kk + 1, :] * inv
+            row_g = row_g * inv
+            gram = gram - col * row_g
+            wide = wide - col * row_w
+        lanes = lax.broadcasted_iota(jnp.int32, (8, size), 1)
+        subl = lax.broadcasted_iota(jnp.int32, (8, size), 0)
+        diag = jnp.sum(jnp.where(lanes == subl + base, gram[:8], 0.0), axis=1, keepdims=True)
+        done.append(wide[:8] * lax.rsqrt(diag))
+        gram, wide = gram[8:], wide[8:]
+    return jnp.concatenate(done, axis=0)
+
+
+def kernel(n, scale, pts, sb, order, mp, mc, pieces, moment, pair_in, half, rs_in, whole,
+           block, out_buf, in_buf, pair_s, pair_r, rs_s, rs_r, ag_s, ag_r, back_s, back_r,
+           ch_s, ch_r, loc):
+    me, sub = lax.axis_index("rows"), lax.axis_index("sub")
+    other = 1 - sub
+    dim, width = pts.shape[0], pts.shape[1] // n
+    hd = dim // 2
+    sl = hd // n
+
+    barrier = pltpu.get_barrier_semaphore()
+    for o in range(1, n):
+        pl.semaphore_signal(barrier, inc=1, device_id={"rows": lax.rem(me + o, n)}, device_id_type=MESH)
+    pl.semaphore_signal(barrier, inc=1, device_id={"sub": other}, device_id_type=MESH)
+
+    x = pts[...]
+    hi = x.astype(jnp.bfloat16)
+    rest = x - hi.astype(jnp.float32)
+    mid = rest.astype(jnp.bfloat16)
+    low = (rest - mid.astype(jnp.float32)).astype(jnp.bfloat16)
+    pieces[0:dim, :] = hi
+    pieces[dim : 2 * dim, :] = mid
+    pieces[2 * dim :, :] = low
+
+    first = lax.dot_general(pieces[...], pieces[0:dim, :], NT, preferred_element_type=jnp.float32)
+    mm = lax.dot_general(pieces[dim : 2 * dim, :], pieces[dim : 2 * dim, :], NT,
+                         preferred_element_type=jnp.float32)
+    cross = first[dim : 2 * dim] + first[2 * dim :]
+    moment[...] = first[0:dim] + ((cross + cross.T) + mm)
+    pl.semaphore_wait(barrier, n)
+
+    def rows_of(which, start_rows, count):
+        return pl.ds(pl.multiple_of(which * start_rows, start_rows), count)
+
+    def remote(src, dst, s, r, **dev):
+        return pltpu.make_async_remote_copy(
+            src_ref=src, dst_ref=dst, send_sem=s, recv_sem=r, device_id=dev, device_id_type=MESH)
+
+    def off(t):
+        return n // 2 + (1 - 2 * (t % 2)) * ((t + 1) // 2)
+
+    def permuted(dest):
+        idx = order[:, pl.ds(pl.multiple_of(dest * width, width), width)]
+        place = lax.broadcasted_iota(jnp.int32, (pts.shape[1], width), 0)
+        hot = jnp.where(place == idx, 1.0, 0.0).astype(jnp.bfloat16)
+        got = jnp.dot(pieces[...], hot, preferred_element_type=jnp.float32)
+        return got[0:dim] + got[dim : 2 * dim] + got[2 * dim :]
+
+    chunk_sends = []
+
+    def chunk(t):
+        dest = lax.rem(me + off(t), n)
+        out_buf[t] = permuted(dest)
+        c = remote(out_buf.at[t], in_buf.at[me], ch_s.at[t], ch_r.at[me], rows=dest)
+        c.start()
+        chunk_sends.append(c)
+
+    pair = remote(moment.at[rows_of(other, hd, hd)], pair_in, pair_s, pair_r, sub=other)
+    pair.start()
+    chunk(0)
+    pair.wait()
+    half[...] = moment[rows_of(sub, hd, hd), :] + pair_in[...]
+    rs = []
+    for o in range(1, n):
+        q = lax.rem(me + o, n)
+        c = remote(half.at[rows_of(q, sl, sl)], rs_in.at[me], rs_s.at[o], rs_r.at[me], rows=q)
+        c.start()
+        rs.append(c)
+    rs_in[me] = half[rows_of(me, sl, sl), :]
+    chunk(1)
+    chunk(2)
+    for o in range(1, n):
+        q = lax.rem(me + o, n)
+        remote(half.at[rows_of(q, sl, sl)], rs_in.at[q], rs_s.at[o], rs_r.at[q], rows=q).wait_recv()
+    mine = pl.ds(pl.multiple_of(sub * hd + me * sl, sl), sl)
+    whole[mine, :] = jnp.sum(rs_in[...], axis=0) * scale
+    ag = []
+    for o in range(1, n):
+        q = lax.rem(me + o, n)
+        c = remote(whole.at[mine], whole.at[mine], ag_s.at[o], ag_r.at[me], rows=q)
+        c.start()
+        ag.append(c)
+    chunk(3)
+    chunk(4)
+    for o in range(1, n):
+        q = lax.rem(me + o, n)
+        theirs = pl.ds(pl.multiple_of(sub * hd + q * sl, sl), sl)
+        remote(whole.at[theirs], whole.at[theirs], ag_s.at[o], ag_r.at[q], rows=q).wait_recv()
+    own_half = rows_of(sub, hd, hd)
+    back = remote(whole.at[own_half], whole.at[own_half], back_s, back_r, sub=other)
+    back.start()
+    for t in range(5, n - 1):
+        chunk(t)
+    in_buf[me] = permuted(me)
+    back.wait()
+
+    block[...] = sb[...].T
+
+    @pl.loop(0, ITERS)
+    def _(step):
+        wide = jnp.dot(block[...], whole[...], precision=HI, preferred_element_type=jnp.float32)
+        gram = lax.dot_general(wide, wide, NT, precision=HI, preferred_element_type=jnp.float32)
+        block[...] = eliminate(gram, wide)
+
+    outs = []
+    for t in list(range(n - 1, n)) + list(range(n - 2, -1, -1)):
+        src = lax.rem(me + n - off(t), n)
+        if t < n - 1:
+            remote(out_buf.at[t], in_buf.at[src], ch_s.at[t], ch_r.at[src], rows=src).wait_recv()
+        cols = pl.ds(pl.multiple_of(src * width, width), width)
+        c = pltpu.make_async_copy(in_buf.at[src], mp.at[:, cols], loc.at[t])
+        c.start()
+        outs.append(c)
+        mc[:, cols] = jnp.dot(block[...], in_buf[src], precision=HI, preferred_element_type=jnp.float32)
+    for c in outs:
+        c.wait()
+    for c in chunk_sends + rs + ag:
+        c.wait_send()
+
+
+def fused(points, start_block, median_order):
+    n = lax.axis_size("rows")
+    dim, count = points.shape
+    k = start_block.shape[1]
+    width, hd = count // n, dim // 2
+    scale = 1.0 / (count * n * lax.axis_size("sub"))
+    f32 = jnp.float32
+    vm, dma = pltpu.VMEM, pltpu.SemaphoreType.DMA
+    return pl.pallas_call(
+        functools.partial(kernel, n, scale),
+        out_shape=(jax.ShapeDtypeStruct((dim, count), f32), jax.ShapeDtypeStruct((k, count), f32)),
+        in_specs=[pl.BlockSpec(memory_space=vm)] * 3,
+        out_specs=(pl.BlockSpec(memory_space=pl.ANY), pl.BlockSpec(memory_space=vm)),
+        scratch_shapes=[
+            vm((3 * dim, count), jnp.bfloat16),
+            vm((dim, dim), f32),
+            vm((hd, dim), f32),
+            vm((hd, dim), f32),
+            vm((n, hd // n, dim), f32),
+            vm((dim, dim), f32),
+            vm((k, dim), f32),
+            vm((n, dim, width), f32),
+            vm((n, dim, width), f32),
+            dma, dma, dma((n,)), dma((n,)), dma((n,)), dma((n,)), dma, dma,
+            dma((n,)), dma((n,)), dma((n,)),
+        ],
+        compiler_params=pltpu.CompilerParams(
+            collective_id=0, has_side_effects=True, vmem_limit_bytes=48 * 1024 * 1024),
+    )(points, start_block, median_order)
+
+
 def solution(mesh):
     in_specs = (
         P("cols", ("groups", "rows", "sub")),
@@ -51,4 +228,6 @@
         P(("groups", "rows", "sub"), None),
     )
     out_specs = (P("cols", ("groups", "rows", "sub")), P(None, ("groups", "rows", "sub")))
-    return jax.shard_map(body, mesh=mesh, in_specs=in_specs, out_specs=out_specs, check_vma=False)
+    whole_features = mesh.shape["cols"] == 1 and mesh.shape["sub"] == 2
+    return jax.shard_map(fused if whole_features else body, mesh=mesh, in_specs=in_specs,
+                         out_specs=out_specs, check_vma=False)

time: 416 us -> 81.4 us (0.20)
  waiting for transfers between devices: 303 us -> 0 us
  Pallas kernels: 0 us -> 75.2 us
  other arithmetic: 41 us -> 0 us
  matrix products: 23.8 us -> 0 us
  local copies, waits for them, and re-layouts: 20.5 us -> 5.33 us
  between operations: 14 us -> 0.65 us
  starting transfers between devices: 12.5 us -> 0 us
    psum x3 -> x0, waiting for transfers between devices: 258 us -> none  [body(): wblock = lax.psum(partial_value, ('rows', 'sub'))]
    pallas_call x0 -> x1, Pallas kernels: none -> 75.2 us  [fused(): pl.pallas_call(functools.partial(kernel, n, scale), out_shape=(jax.ShapeD...]
    all_to_all x2 -> x0, waiting for transfers between devices: 45.1 us -> none  [the longest x1 45.1 us: body(): lax.all_to_all(sent_points, 'rows', split_axis=1, concat_axis=1, tiled=True)]
    another operation x15 -> x0, other arithmetic: 36.2 us -> none  [the longest x9 19.6 us: orthonormal(): lower = jnp.linalg.cholesky(gram)]
    dot_general x10 -> x0, matrix products: 20.5 us -> none  [the longest x4 9.15 us: project(): return lax.psum(jnp.dot(block.T, points, precision=HI), 'cols')]
    gather x3 -> x0, local copies, waits for them, and re-layouts: 14.4 us -> none  [the longest x1 8.61 us: body(): sent_points = jnp.take(points, order, axis=1)]
    all_to_all x2 -> x0, starting transfers between devices: 12.2 us -> none  [the longest x1 6.19 us: body(): lax.all_to_all(sent_coords, 'rows', split_axis=1, concat_axis=1, tiled=True)]
  transfers between devices with their start and end apart: 5 -> 0, of which waited for: 4 -> 0; matrix products, arithmetic and copies ran while one was open for 4% -> 0% of each run, Pallas kernels for 0% -> 0%
where the time goes in v1:
time: 81.4 us; the launch traced here: 81.2 us
  Pallas kernels  75.2 us (92%)
  local copies, waits for them, and re-layouts  5.33 us (7%)
    pallas_call x1, Pallas kernels, fused(): pl.pallas_call(functools.partial(kernel, n, scale), out_shape=(jax.ShapeD...  75.2 us
    unnamed x7, local copies, waits for them, and re-layouts  5.33 us

profile of v1, /device:TPU:0, one launch (start us, length us, event | category | flops | bytes accessed | tf_op | source)
XLA Modules:
  0.0 81.2 jit_solution(3467277253651166475)
XLA Ops:
  0.6 0.9 %copy.5.sb = f32[256,64]{1,0:T(8,128)S(1)} copy(f32[256,64]{0,1:T(8,128)} %param.4) | data formatting | bytes 131072 | tf_op args[1]
  1.6 0.0 copy-start
  1.6 1.6 %copy-done = f32[256,2048]{1,0:T(8,128)S(1)} copy-done((f32[256,2048]{1,0:T(8,128)S(1)}, f32[256,2048]{1,0:T(8,128)}, u32[]{:S(2)}) %copy-start) | copy-done | bytes 2097176
  3.2 0.0 copy-start.1
  3.2 0.7 copy-done.1
  3.9 75.2 %shard_map.50 = (f32[256,2048]{1,0:T(8,128)S(1)}, f32[64,2048]{1,0:T(8,128)S(1)}) custom-call(f32[256,2048]{1,0:T(8,128)S(1)} %copy-done, f32[256,64]{1,0:T(8,128)S(1)} %copy.5.sb, s32[1,2048]{1,0:T(1,128)S(1)} %copy-done.1), custom_call_target="tpu_custom_call" | custom-call | tf_op jit(solution)/shard_map/pallas_call | solution.py:201
  79.1 1.3 %copy.8 = f32[256,2048]{1,0:T(8,128)} copy(f32[256,2048]{1,0:T(8,128)S(1)} %get-tuple-element.4) | data formatting | bytes 4194304
  80.4 0.8 copy.9
Async XLA Ops:
  1.6 1.6 %copy-start = (f32[256,2048]{1,0:T(8,128)S(1)}, f32[256,2048]{1,0:T(8,128)}, u32[]{:S(2)}) copy-start(f32[256,2048]{1,0:T(8,128)} %pts.1) | copy-start | bytes 6291460
  3.2 0.7 copy-start.1

commit v2 on v1

--- a/solution.py
+++ b/solution.py
@@ -10,6 +10,8 @@
 
 
 HI = lax.Precision.HIGHEST
+EARLY, MIDDLE, LATE = 1, 1, 2
+ORDERS = ((4, 2, 6, 3, 5, 1, 7), (2, 4, 3, 6, 1, 5, 7))
 MESH = pl.DeviceIdType.MESH
 NT = (((1,), (1,)), ((), ()))
 
@@ -71,34 +73,37 @@
     return jnp.concatenate(done, axis=0)
 
 
-def kernel(n, scale, pts, sb, order, mp, mc, pieces, moment, pair_in, half, rs_in, whole,
+def kernel(n, scale, pts_hbm, sb, order, mp, mc, pieces, moment, pair_in, half, rs_in, whole,
            block, out_buf, in_buf, pair_s, pair_r, rs_s, rs_r, ag_s, ag_r, back_s, back_r,
-           ch_s, ch_r, loc):
+           ch_s, ch_r, loc, pts, ld):
     me, sub = lax.axis_index("rows"), lax.axis_index("sub")
     other = 1 - sub
     dim, width = pts.shape[0], pts.shape[1] // n
     hd = dim // 2
     sl = hd // n
 
+    loads = []
+    for i in range(n):
+        c = pltpu.make_async_copy(pts_hbm.at[:, i * width : (i + 1) * width],
+                                  pts.at[:, i * width : (i + 1) * width], ld.at[i])
+        c.start()
+        loads.append(c)
+
     barrier = pltpu.get_barrier_semaphore()
     for o in range(1, n):
         pl.semaphore_signal(barrier, inc=1, device_id={"rows": lax.rem(me + o, n)}, device_id_type=MESH)
     pl.semaphore_signal(barrier, inc=1, device_id={"sub": other}, device_id_type=MESH)
 
-    x = pts[...]
-    hi = x.astype(jnp.bfloat16)
-    rest = x - hi.astype(jnp.float32)
-    mid = rest.astype(jnp.bfloat16)
-    low = (rest - mid.astype(jnp.float32)).astype(jnp.bfloat16)
-    pieces[0:dim, :] = hi
-    pieces[dim : 2 * dim, :] = mid
-    pieces[2 * dim :, :] = low
-
-    first = lax.dot_general(pieces[...], pieces[0:dim, :], NT, preferred_element_type=jnp.float32)
-    mm = lax.dot_general(pieces[dim : 2 * dim, :], pieces[dim : 2 * dim, :], NT,
-                         preferred_element_type=jnp.float32)
-    cross = first[dim : 2 * dim] + first[2 * dim :]
-    moment[...] = first[0:dim] + ((cross + cross.T) + mm)
+    for i in range(n):
+        part = pl.ds(i * width, width)
+        loads[i].wait()
+        x = pts[:, part]
+        hi = x.astype(jnp.bfloat16)
+        rest = x - hi.astype(jnp.float32)
+        mid = rest.astype(jnp.bfloat16)
+        pieces[0:dim, part] = hi
+        pieces[dim : 2 * dim, part] = mid
+        pieces[2 * dim :, part] = (rest - mid.astype(jnp.float32)).astype(jnp.bfloat16)
     pl.semaphore_wait(barrier, n)
 
     def rows_of(which, start_rows, count):
@@ -108,8 +113,14 @@
         return pltpu.make_async_remote_copy(
             src_ref=src, dst_ref=dst, send_sem=s, recv_sem=r, device_id=dev, device_id_type=MESH)
 
-    def off(t):
-        return n // 2 + (1 - 2 * (t % 2)) * ((t + 1) // 2)
+    def peer(t):
+        first_c, second_c = ORDERS[0][t], ORDERS[1][t]
+        c = first_c + sub * (second_c - first_c)
+        dest, bit = me, 1
+        while bit < n:
+            dest = dest + lax.rem(c // bit, 2) * (1 - 2 * lax.rem(me // bit, 2)) * bit
+            bit *= 2
+        return dest
 
     def permuted(dest):
         idx = order[:, pl.ds(pl.multiple_of(dest * width, width), width)]
@@ -120,16 +131,26 @@
 
     chunk_sends = []
 
-    def chunk(t):
-        dest = lax.rem(me + off(t), n)
-        out_buf[t] = permuted(dest)
+    def permute(t):
+        out_buf[t] = permuted(peer(t))
+
+    def send(t):
+        dest = peer(t)
         c = remote(out_buf.at[t], in_buf.at[me], ch_s.at[t], ch_r.at[me], rows=dest)
         c.start()
         chunk_sends.append(c)
 
+    for t in range(EARLY):
+        permute(t)
+        send(t)
+    first = lax.dot_general(pieces[...], pieces[0:dim, :], NT, preferred_element_type=jnp.float32)
+    mm = lax.dot_general(pieces[dim : 2 * dim, :], pieces[dim : 2 * dim, :], NT,
+                         preferred_element_type=jnp.float32)
+    cross = first[dim : 2 * dim] + first[2 * dim :]
+    moment[...] = first[0:dim] + ((cross + cross.T) + mm)
     pair = remote(moment.at[rows_of(other, hd, hd)], pair_in, pair_s, pair_r, sub=other)
     pair.start()
-    chunk(0)
+    permute(EARLY)
     pair.wait()
     half[...] = moment[rows_of(sub, hd, hd), :] + pair_in[...]
     rs = []
@@ -139,8 +160,10 @@
         c.start()
         rs.append(c)
     rs_in[me] = half[rows_of(me, sl, sl), :]
-    chunk(1)
-    chunk(2)
+    for t in range(EARLY, MIDDLE):
+        send(t)
+    for t in range(EARLY + 1, n - 1):
+        permute(t)
     for o in range(1, n):
         q = lax.rem(me + o, n)
         remote(half.at[rows_of(q, sl, sl)], rs_in.at[q], rs_s.at[o], rs_r.at[q], rows=q).wait_recv()
@@ -152,8 +175,10 @@
         c = remote(whole.at[mine], whole.at[mine], ag_s.at[o], ag_r.at[me], rows=q)
         c.start()
         ag.append(c)
-    chunk(3)
-    chunk(4)
+    for t in range(MIDDLE, LATE):
+        send(t)
+    in_buf[me] = permuted(me)
+    block[...] = sb[...].T
     for o in range(1, n):
         q = lax.rem(me + o, n)
         theirs = pl.ds(pl.multiple_of(sub * hd + q * sl, sl), sl)
@@ -161,12 +186,9 @@
     own_half = rows_of(sub, hd, hd)
     back = remote(whole.at[own_half], whole.at[own_half], back_s, back_r, sub=other)
     back.start()
-    for t in range(5, n - 1):
-        chunk(t)
-    in_buf[me] = permuted(me)
+    for t in range(LATE, n - 1):
+        send(t)
     back.wait()
-
-    block[...] = sb[...].T
 
     @pl.loop(0, ITERS)
     def _(step):
@@ -175,8 +197,8 @@
         block[...] = eliminate(gram, wide)
 
     outs = []
-    for t in list(range(n - 1, n)) + list(range(n - 2, -1, -1)):
-        src = lax.rem(me + n - off(t), n)
+    for t in [n - 1] + list(range(n - 1)):
+        src = me if t == n - 1 else peer(t)
         if t < n - 1:
             remote(out_buf.at[t], in_buf.at[src], ch_s.at[t], ch_r.at[src], rows=src).wait_recv()
         cols = pl.ds(pl.multiple_of(src * width, width), width)
@@ -201,7 +223,7 @@
     return pl.pallas_call(
         functools.partial(kernel, n, scale),
         out_shape=(jax.ShapeDtypeStruct((dim, count), f32), jax.ShapeDtypeStruct((k, count), f32)),
-        in_specs=[pl.BlockSpec(memory_space=vm)] * 3,
+        in_specs=[pl.BlockSpec(memory_space=pl.ANY)] + [pl.BlockSpec(memory_space=vm)] * 2,
         out_specs=(pl.BlockSpec(memory_space=pl.ANY), pl.BlockSpec(memory_space=vm)),
         scratch_shapes=[
             vm((3 * dim, count), jnp.bfloat16),
@@ -215,6 +237,7 @@
             vm((n, dim, width), f32),
             dma, dma, dma((n,)), dma((n,)), dma((n,)), dma((n,)), dma, dma,
             dma((n,)), dma((n,)), dma((n,)),
+            vm((dim, count), f32), dma((n,)),
         ],
         compiler_params=pltpu.CompilerParams(
             collective_id=0, has_side_effects=True, vmem_limit_bytes=48 * 1024 * 1024),
@@ -228,6 +251,7 @@
         P(("groups", "rows", "sub"), None),
     )
     out_specs = (P("cols", ("groups", "rows", "sub")), P(None, ("groups", "rows", "sub")))
-    whole_features = mesh.shape["cols"] == 1 and mesh.shape["sub"] == 2
+    peers = len(ORDERS[0])
+    whole_features = mesh.shape["cols"] == 1 and mesh.shape["sub"] == 2 and mesh.shape["rows"] == peers + 1
     return jax.shard_map(fused if whole_features else body, mesh=mesh, in_specs=in_specs,
                          out_specs=out_specs, check_vma=False)

time: 81.4 us -> 67.2 us (0.83)
  Pallas kernels: 75.2 us -> 60.9 us
    pallas_call x1, Pallas kernels: 75.2 us -> 60.9 us  [fused(): pl.pallas_call(functools.partial(kernel, n, scale), out_shape=(jax.ShapeD...]
where the time goes in v2:
time: 67.2 us; the launch traced here: 66.9 us
  Pallas kernels  60.9 us (91%)
  local copies, waits for them, and re-layouts  5.33 us (8%)
    pallas_call x1, Pallas kernels, fused(): pl.pallas_call(functools.partial(kernel, n, scale), out_shape=(jax.ShapeD...  60.9 us
    unnamed x7, local copies, waits for them, and re-layouts  5.33 us

profile of v2, /device:TPU:0, one launch (start us, length us, event | category | flops | bytes accessed | tf_op | source)
XLA Modules:
  0.0 66.9 jit_solution(13488207585653161782)
XLA Ops:
  0.6 0.9 %copy.5.sb = f32[256,64]{1,0:T(8,128)S(1)} copy(f32[256,64]{0,1:T(8,128)} %param.4) | data formatting | bytes 131072 | tf_op args[1]
  1.6 0.0 copy-start
  1.6 1.6 %copy-done = f32[256,2048]{1,0:T(8,128)S(1)} copy-done((f32[256,2048]{1,0:T(8,128)S(1)}, f32[256,2048]{1,0:T(8,128)}, u32[]{:S(2)}) %copy-start) | copy-done | bytes 2097176
  3.2 0.0 copy-start.1
  3.2 0.7 %copy-done.1 = s32[1,2048]{1,0:T(1,128)S(1)} copy-done((s32[1,2048]{1,0:T(1,128)S(1)}, s32[1,2048]{1,0:T(1,128)}, u32[]{:S(2)}) %copy-start.1) | copy-done | bytes 8216
  3.9 60.9 %shard_map.50 = (f32[256,2048]{1,0:T(8,128)S(1)}, f32[64,2048]{1,0:T(8,128)S(1)}) custom-call(f32[256,2048]{1,0:T(8,128)S(1)} %copy-done, f32[256,64]{1,0:T(8,128)S(1)} %copy.5.sb, s32[1,2048]{1,0:T(1,128)S(1)} %copy-done.1), custom_call_target="tpu_custom_call" | custom-call | tf_op jit(solution)/shard_map/pallas_call | solution.py:223
  64.8 1.3 %copy.8 = f32[256,2048]{1,0:T(8,128)} copy(f32[256,2048]{1,0:T(8,128)S(1)} %get-tuple-element.4) | data formatting | bytes 4194304
  66.1 0.8 %copy.9 = f32[64,2048]{1,0:T(8,128)} copy(f32[64,2048]{1,0:T(8,128)S(1)} %get-tuple-element.5) | data formatting | bytes 1048576
Async XLA Ops:
  1.6 1.6 %copy-start = (f32[256,2048]{1,0:T(8,128)S(1)}, f32[256,2048]{1,0:T(8,128)}, u32[]{:S(2)}) copy-start(f32[256,2048]{1,0:T(8,128)} %pts_hbm.1) | copy-start | bytes 6291460
  3.2 0.7 %copy-start.1 = (s32[1,2048]{1,0:T(1,128)S(1)}, s32[1,2048]{1,0:T(1,128)}, u32[]{:S(2)}) copy-start(s32[1,2048]{1,0:T(1,128)} %order.1) | copy-start | bytes 24580

commit v3 on v2

--- a/solution.py
+++ b/solution.py
@@ -10,7 +10,7 @@
 
 
 HI = lax.Precision.HIGHEST
-EARLY, MIDDLE, LATE = 1, 1, 2
+EARLY, MIDDLE, LATE = 1, 1, 3
 ORDERS = ((4, 2, 6, 3, 5, 1, 7), (2, 4, 3, 6, 1, 5, 7))
 MESH = pl.DeviceIdType.MESH
 NT = (((1,), (1,)), ((), ()))

time: 67.2 us -> 66.8 us (level)
  Pallas kernels: 60.9 us -> 60.1 us
    pallas_call x1, Pallas kernels: 60.9 us -> 60.1 us  [fused(): pl.pallas_call(functools.partial(kernel, n, scale), out_shape=(jax.ShapeD...]
where the time goes in v3:
time: 66.8 us; the launch traced here: 66.1 us
  Pallas kernels  60.1 us (90%)
  local copies, waits for them, and re-layouts  5.33 us (8%)
    pallas_call x1, Pallas kernels, fused(): pl.pallas_call(functools.partial(kernel, n, scale), out_shape=(jax.ShapeD...  60.1 us
    unnamed x7, local copies, waits for them, and re-layouts  5.33 us

profile of v3, /device:TPU:0, one launch (start us, length us, event | category | flops | bytes accessed | tf_op | source)
XLA Modules:
  0.0 66.1 jit_solution(7423046979985686126)
XLA Ops:
  0.6 0.9 %copy.5.sb = f32[256,64]{1,0:T(8,128)S(1)} copy(f32[256,64]{0,1:T(8,128)} %param.4) | data formatting | bytes 131072 | tf_op args[1]
  1.6 0.0 copy-start
  1.6 1.6 %copy-done = f32[256,2048]{1,0:T(8,128)S(1)} copy-done((f32[256,2048]{1,0:T(8,128)S(1)}, f32[256,2048]{1,0:T(8,128)}, u32[]{:S(2)}) %copy-start) | copy-done | bytes 2097176
  3.2 0.0 copy-start.1
  3.2 0.7 %copy-done.1 = s32[1,2048]{1,0:T(1,128)S(1)} copy-done((s32[1,2048]{1,0:T(1,128)S(1)}, s32[1,2048]{1,0:T(1,128)}, u32[]{:S(2)}) %copy-start.1) | copy-done | bytes 8216
  3.9 60.1 %shard_map.50 = (f32[256,2048]{1,0:T(8,128)S(1)}, f32[64,2048]{1,0:T(8,128)S(1)}) custom-call(f32[256,2048]{1,0:T(8,128)S(1)} %copy-done, f32[256,64]{1,0:T(8,128)S(1)} %copy.5.sb, s32[1,2048]{1,0:T(1,128)S(1)} %copy-done.1), custom_call_target="tpu_custom_call" | custom-call | tf_op jit(solution)/shard_map/pallas_call | solution.py:223
  64.0 1.3 %copy.8 = f32[256,2048]{1,0:T(8,128)} copy(f32[256,2048]{1,0:T(8,128)S(1)} %get-tuple-element.4) | data formatting | bytes 4194304
  65.3 0.8 %copy.9 = f32[64,2048]{1,0:T(8,128)} copy(f32[64,2048]{1,0:T(8,128)S(1)} %get-tuple-element.5) | data formatting | bytes 1048576
Async XLA Ops:
  1.6 1.6 %copy-start = (f32[256,2048]{1,0:T(8,128)S(1)}, f32[256,2048]{1,0:T(8,128)}, u32[]{:S(2)}) copy-start(f32[256,2048]{1,0:T(8,128)} %pts_hbm.1) | copy-start | bytes 6291460
  3.2 0.7 %copy-start.1 = (s32[1,2048]{1,0:T(1,128)S(1)}, s32[1,2048]{1,0:T(1,128)}, u32[]{:S(2)}) copy-start(s32[1,2048]{1,0:T(1,128)} %order.1) | copy-start | bytes 24580
